TPU v7x, 32 devices: a whole 2x2x4 slice. The times are simulated.
32 devices in a mesh: dp: 16 (over z, y, x), tensor: 2 (over core).
Axes of the slice: x: 2, y: 2, z: 4, core: 2. Of those that a mesh axis runs over, the one named last changes fastest.
Arguments:
- tokens: bfloat16 [32768, 640], P(('dp', 'tensor')), may hold values from -6 to 6
- w_query: bfloat16 [640, 1024], P('dp', 'tensor'), may hold values from -0.25 to 0.25
- w_key: bfloat16 [640, 256], P('dp'), may hold values from -0.25 to 0.25
- w_value: bfloat16 [640, 256], P('dp'), may hold values from -0.25 to 0.25
- w_out: bfloat16 [1024, 640], P('tensor', 'dp'), may hold values from -0.1875 to 0.1875
- gain_attn: bfloat16 [640], P('dp'), may hold values from 0.5 to 1.5
- gain_query: bfloat16 [256], P('dp'), may hold values from 0.5 to 1.5
- gain_key: bfloat16 [256], P('dp'), may hold values from 0.5 to 1.5
- gain_post_attn: bfloat16 [640], P('dp'), may hold values from 0.5 to 1.5
- w_gate: bfloat16 [640, 2048], P('dp', 'tensor'), may hold values from -0.25 to 0.25
- w_up: bfloat16 [640, 2048], P('dp', 'tensor'), may hold values from -0.25 to 0.25
- w_down: bfloat16 [2048, 640], P('tensor', 'dp'), may hold values from -0.125 to 0.125
- gain_pre_ffn: bfloat16 [640], P('dp'), may hold values from 0.5 to 1.5
- gain_post_ffn: bfloat16 [640], P('dp'), may hold values from 0.5 to 1.5
- cotangent: bfloat16 [32768, 640], P(('dp', 'tensor')), may hold values from -6 to 6
Outputs:
- output: bfloat16 [32768, 640], P(('dp', 'tensor'))
- tokens_grad: float32 [32768, 640], P(('dp', 'tensor'))
- w_query_grad: float32 [640, 1024], P('dp', 'tensor')
- w_key_grad: float32 [640, 256], P('dp')
- w_value_grad: float32 [640, 256], P('dp')
- w_out_grad: float32 [1024, 640], P('tensor', 'dp')
- gain_attn_grad: float32 [640], P('dp')
- gain_query_grad: float32 [256], P('dp')
- gain_key_grad: float32 [256], P('dp')
- gain_post_attn_grad: float32 [640], P('dp')
- w_gate_grad: float32 [640, 2048], P('dp', 'tensor')
- w_up_grad: float32 [640, 2048], P('dp', 'tensor')
- w_down_grad: float32 [2048, 640], P('tensor', 'dp')
- gain_pre_ffn_grad: float32 [640], P('dp')
- gain_post_ffn_grad: float32 [640], P('dp')
All inputs are finite; a program needn't handle non-finite values.
Results may differ from a plain program's by a relative error of at most 0.018.
Values may be sent and summed in bfloat16 or wider, within the bound.
A program may use at most 192 MiB of HBM per device.

v0:
```python
import math

import jax
import jax.numpy as jnp
from jax import lax
from jax.sharding import PartitionSpec as P

EPS = 1e-06
MASKED = -1e30


def matmul(left, right):
    return jnp.dot(left, right, preferred_element_type=jnp.float32)


def times_transposed(left, right):
    return lax.dot_general(
        left, right, (((1,), (1,)), ((), ())), preferred_element_type=jnp.float32
    )


def transposed_times(left, right):
    return lax.dot_general(
        left, right, (((0,), (0,)), ((), ())), preferred_element_type=jnp.float32
    )


def norm_rows(value, gain):
    scale = lax.rsqrt(jnp.mean(value * value, axis=-1, keepdims=True) + EPS)
    unit = value * scale
    return (unit * gain, unit, scale)


def norm_back(grad, unit, scale, gain, axes):
    gain_grad = jnp.sum(grad * unit, axis=axes)
    inner = grad * gain
    return (scale * (inner - unit * jnp.mean(inner * unit, axis=-1, keepdims=True)), gain_grad)


def tables(positions, width):
    half = width // 2
    freqs = jnp.exp(jnp.arange(half, dtype=jnp.float32) * (-2.0 * math.log(1000000.0) / width))
    angles = positions.astype(jnp.float32)[:, None] * freqs[None, :]
    angles = jnp.concatenate([angles, angles], axis=1)
    return (jnp.cos(angles), jnp.sin(angles))


def turn(value, cosine, sine):
    half = value.shape[-1] // 2
    rotated = jnp.concatenate([-value[..., half:], value[..., :half]], axis=-1)
    return value * cosine + rotated * sine


def turn_back(grad, cosine, sine):
    half = grad.shape[-1] // 2
    moved = grad * sine
    return grad * cosine + jnp.concatenate([moved[..., half:], -moved[..., :half]], axis=-1)


def gelu_tanh(value):
    return jax.nn.gelu(value, approximate=True)


def per_device(
    tokens,
    w_query,
    w_key,
    w_value,
    w_out,
    gain_attn,
    gain_query,
    gain_key,
    gain_post_attn,
    w_gate,
    w_up,
    w_down,
    gain_pre_ffn,
    gain_post_ffn,
    cotangent,
):
    parts = lax.axis_size("tensor")
    own_rows = tokens.shape[0]
    length = own_rows * parts
    head_dim = w_key.shape[1]
    factor = head_dim ** (-0.5)
    gathered = (
        lax.all_gather(w_query, "dp", axis=0, tiled=True),
        lax.all_gather(w_key, "dp", axis=0, tiled=True),
        lax.all_gather(w_value, "dp", axis=0, tiled=True),
        lax.all_gather(w_out, "dp", axis=1, tiled=True),
        lax.all_gather(gain_attn, "dp", axis=0, tiled=True),
        lax.all_gather(gain_query, "dp", axis=0, tiled=True),
        lax.all_gather(gain_key, "dp", axis=0, tiled=True),
        lax.all_gather(gain_post_attn, "dp", axis=0, tiled=True),
        lax.all_gather(w_gate, "dp", axis=0, tiled=True),
        lax.all_gather(w_up, "dp", axis=0, tiled=True),
        lax.all_gather(w_down, "dp", axis=1, tiled=True),
        lax.all_gather(gain_pre_ffn, "dp", axis=0, tiled=True),
        lax.all_gather(gain_post_ffn, "dp", axis=0, tiled=True),
    )
    query_w, key_w, value_w, out_w = (gathered[0], gathered[1], gathered[2], gathered[3])
    attn_g = gathered[4].astype(jnp.float32)
    query_g = gathered[5].astype(jnp.float32)
    key_g = gathered[6].astype(jnp.float32)
    post_attn_g = gathered[7].astype(jnp.float32)
    gate_w, up_w, down_w = (gathered[8], gathered[9], gathered[10])
    pre_ffn_g = gathered[11].astype(jnp.float32)
    post_ffn_g = gathered[12].astype(jnp.float32)
    offset = lax.axis_index("tensor") * own_rows
    own_cos, own_sin = tables(offset + jnp.arange(own_rows, dtype=jnp.int32), head_dim)
    inputs = tokens.astype(jnp.float32)
    normed, attn_unit, attn_scale = norm_rows(inputs, attn_g)
    normed_low = normed.astype(jnp.bfloat16)
    key_pre = matmul(normed_low, key_w)
    value_low = matmul(normed_low, value_w).astype(jnp.bfloat16)
    key_normed, key_unit, key_scale = norm_rows(key_pre, key_g)
    key_low = turn(key_normed, own_cos, own_sin).astype(jnp.bfloat16)
    query_rows, key_full, value_full = (
        lax.all_gather(normed_low, "tensor", axis=0, tiled=True),
        lax.all_gather(key_low, "tensor", axis=0, tiled=True),
        lax.all_gather(value_low, "tensor", axis=0, tiled=True),
    )
    query_w_use, out_w_use = (query_w, out_w)
    query_cos, query_sin = tables(jnp.arange(length, dtype=jnp.int32), head_dim)
    query_count = query_rows.shape[0]
    query_heads = query_w_use.shape[1] // head_dim
    block = min(512, query_count)
    blocks = query_count // block
    query_pre = matmul(query_rows, query_w_use).reshape(query_count, query_heads, head_dim)
    query_normed, query_unit, query_scale = norm_rows(query_pre, query_g)
    query_low = turn(query_normed, query_cos[:, None, :], query_sin[:, None, :]).astype(
        jnp.bfloat16
    )
    key_places = jnp.arange(length, dtype=jnp.int32)

    def scores_of(query_block, start):
        scores = (
            jnp.einsum("qhd,kd->hqk", query_block, key_full, preferred_element_type=jnp.float32)
            * factor
        )
        places = start + jnp.arange(block, dtype=jnp.int32)
        allowed = places[:, None] >= key_places[None, :]
        return jnp.where(allowed[None], scores, MASKED)

    def forward_block(number):
        start = number * block
        query_block = lax.dynamic_slice_in_dim(query_low, start, block, 0)
        scores = scores_of(query_block, start)
        peak = jnp.max(scores, axis=-1, keepdims=True)
        expon = jnp.exp(scores - peak)
        totals = jnp.sum(expon, axis=-1, keepdims=True)
        prob = expon / totals
        mixed_block = jnp.einsum(
            "hqk,kd->qhd", prob.astype(jnp.bfloat16), value_full, preferred_element_type=jnp.float32
        )
        return (mixed_block.astype(jnp.bfloat16), (peak + jnp.log(totals))[..., 0])

    mixed_blocks, log_totals = lax.map(forward_block, jnp.arange(blocks, dtype=jnp.int32))
    mixed = mixed_blocks.reshape(query_count, query_heads * head_dim)
    attn_sum = lax.psum_scatter(matmul(mixed, out_w_use), "tensor", scatter_dimension=0, tiled=True)
    attn_branch, post_attn_unit, post_attn_scale = norm_rows(attn_sum, post_attn_g)
    middle = inputs + attn_branch
    ffn_normed, pre_ffn_unit, pre_ffn_scale = norm_rows(middle, pre_ffn_g)
    ffn_low = ffn_normed.astype(jnp.bfloat16)
    ffn_rows = lax.all_gather(ffn_low, "tensor", axis=0, tiled=True)
    gate_use, up_use, down_use = (gate_w, up_w, down_w)
    gate = matmul(ffn_rows, gate_use)
    up = matmul(ffn_rows, up_use)
    activated, gelu_pull = jax.vjp(gelu_tanh, gate)
    hidden = (activated * up).astype(jnp.bfloat16)
    ffn_sum = lax.psum_scatter(matmul(hidden, down_use), "tensor", scatter_dimension=0, tiled=True)
    ffn_branch, post_ffn_unit, post_ffn_scale = norm_rows(ffn_sum, post_ffn_g)
    output = (middle + ffn_branch).astype(jnp.bfloat16)
    out_grad = cotangent.astype(jnp.float32)
    ffn_sum_grad, post_ffn_gain_grad = norm_back(
        out_grad, post_ffn_unit, post_ffn_scale, post_ffn_g, 0
    )
    ffn_sum_low = ffn_sum_grad.astype(jnp.bfloat16)
    ffn_grad_rows = lax.all_gather(ffn_sum_low, "tensor", axis=0, tiled=True)
    hidden_grad = times_transposed(ffn_grad_rows, down_use)
    down_w_grad = transposed_times(hidden, ffn_grad_rows)
    gate_grad = gelu_pull(hidden_grad * up)[0].astype(jnp.bfloat16)
    up_grad = (hidden_grad * activated).astype(jnp.bfloat16)
    gate_w_grad = transposed_times(ffn_rows, gate_grad)
    up_w_grad = transposed_times(ffn_rows, up_grad)
    ffn_in_grad = lax.psum_scatter(
        times_transposed(gate_grad, gate_use) + times_transposed(up_grad, up_use),
        "tensor",
        scatter_dimension=0,
        tiled=True,
    )
    middle_part, pre_ffn_gain_grad = norm_back(
        ffn_in_grad, pre_ffn_unit, pre_ffn_scale, pre_ffn_g, 0
    )
    gate_owned, up_owned, down_owned = (
        lax.psum_scatter(gate_w_grad, "dp", scatter_dimension=0, tiled=True),
        lax.psum_scatter(up_w_grad, "dp", scatter_dimension=0, tiled=True),
        lax.psum_scatter(down_w_grad, "dp", scatter_dimension=1, tiled=True),
    )
    middle_grad = out_grad + middle_part
    attn_sum_grad, post_attn_gain_grad = norm_back(
        middle_grad, post_attn_unit, post_attn_scale, post_attn_g, 0
    )
    attn_sum_low = attn_sum_grad.astype(jnp.bfloat16)
    attn_grad_rows = lax.all_gather(attn_sum_low, "tensor", axis=0, tiled=True)
    out_w_grad = transposed_times(mixed, attn_grad_rows)
    mixed_grad = times_transposed(attn_grad_rows, out_w_use).astype(jnp.bfloat16)
    mixed_grad_heads = mixed_grad.reshape(query_count, query_heads, head_dim)

    def backward_block(carry, number):
        key_grad, value_grad = carry
        start = number * block
        query_block = lax.dynamic_slice_in_dim(query_low, start, block, 0)
        grad_block = lax.dynamic_slice_in_dim(mixed_grad_heads, start, block, 0)
        scores = scores_of(query_block, start)
        prob = jnp.exp(scores - log_totals[number][..., None])
        prob_grad = jnp.einsum(
            "qhd,kd->hqk", grad_block, value_full, preferred_element_type=jnp.float32
        )
        weighted = jnp.sum(prob * prob_grad, axis=-1, keepdims=True)
        score_grad = (prob * (prob_grad - weighted)).astype(jnp.bfloat16)
        query_grad = (
            jnp.einsum("hqk,kd->qhd", score_grad, key_full, preferred_element_type=jnp.float32)
            * factor
        )
        key_grad = (
            key_grad
            + jnp.einsum("hqk,qhd->kd", score_grad, query_block, preferred_element_type=jnp.float32)
            * factor
        )
        value_grad = value_grad + jnp.einsum(
            "hqk,qhd->kd", prob.astype(jnp.bfloat16), grad_block, preferred_element_type=jnp.float32
        )
        return ((key_grad, value_grad), query_grad)

    zeros = jnp.zeros((length, head_dim), jnp.float32)
    (key_grad, value_grad), query_grads = lax.scan(
        backward_block, (zeros, zeros), jnp.arange(blocks, dtype=jnp.int32)
    )
    query_grad = query_grads.reshape(query_count, query_heads, head_dim)
    query_turned = turn_back(query_grad, query_cos[:, None, :], query_sin[:, None, :])
    query_pre_grad, query_gain_grad = norm_back(
        query_turned, query_unit, query_scale, query_g, (0, 1)
    )
    query_low_grad = query_pre_grad.astype(jnp.bfloat16).reshape(
        query_count, query_heads * head_dim
    )
    query_w_grad = transposed_times(query_rows, query_low_grad)
    normed_term = times_transposed(query_low_grad, query_w_use)
    key_value_term = jnp.concatenate([key_grad, value_grad], axis=1)
    normed_grad, key_value_grad = (
        lax.psum_scatter(
            normed_term.astype(jnp.bfloat16), "tensor", scatter_dimension=0, tiled=True
        ).astype(jnp.float32),
        lax.psum_scatter(
            key_value_term.astype(jnp.bfloat16), "tensor", scatter_dimension=0, tiled=True
        ).astype(jnp.float32),
    )
    key_turned = turn_back(key_value_grad[:, :head_dim], own_cos, own_sin)
    key_pre_grad, key_gain_grad = norm_back(key_turned, key_unit, key_scale, key_g, 0)
    key_low_grad = key_pre_grad.astype(jnp.bfloat16)
    value_low_grad = key_value_grad[:, head_dim:].astype(jnp.bfloat16)
    key_w_grad = transposed_times(normed_low, key_low_grad)
    value_w_grad = transposed_times(normed_low, value_low_grad)
    normed_grad = (
        normed_grad
        + times_transposed(key_low_grad, key_w)
        + times_transposed(value_low_grad, value_w)
    )
    input_part, attn_gain_grad = norm_back(normed_grad, attn_unit, attn_scale, attn_g, 0)
    tokens_grad = middle_grad + input_part
    owned = (
        lax.psum_scatter(query_w_grad, "dp", scatter_dimension=0, tiled=True),
        lax.psum_scatter(key_w_grad, "dp", scatter_dimension=0, tiled=True),
        lax.psum_scatter(value_w_grad, "dp", scatter_dimension=0, tiled=True),
        lax.psum_scatter(out_w_grad, "dp", scatter_dimension=1, tiled=True),
        lax.psum_scatter(attn_gain_grad, "dp", scatter_dimension=0, tiled=True),
        lax.psum_scatter(query_gain_grad, "dp", scatter_dimension=0, tiled=True),
        lax.psum_scatter(key_gain_grad, "dp", scatter_dimension=0, tiled=True),
        lax.psum_scatter(post_attn_gain_grad, "dp", scatter_dimension=0, tiled=True),
        lax.psum_scatter(pre_ffn_gain_grad, "dp", scatter_dimension=0, tiled=True),
        lax.psum_scatter(post_ffn_gain_grad, "dp", scatter_dimension=0, tiled=True),
    )
    shared = lax.psum(
        (owned[1], owned[2], owned[4], owned[5], owned[6], owned[7], owned[8], owned[9]), "tensor"
    )
    return (
        output,
        tokens_grad,
        owned[0],
        shared[0],
        shared[1],
        owned[3],
        shared[2],
        shared[3],
        shared[4],
        shared[5],
        gate_owned,
        up_owned,
        down_owned,
        shared[6],
        shared[7],
    )


def solution(mesh):
    return jax.shard_map(
        per_device,
        mesh=mesh,
        in_specs=(
            P(("dp", "tensor"), None),
            P("dp", "tensor"),
            P("dp", None),
            P("dp", None),
            P("tensor", "dp"),
            P("dp"),
            P("dp"),
            P("dp"),
            P("dp"),
            P("dp", "tensor"),
            P("dp", "tensor"),
            P("tensor", "dp"),
            P("dp"),
            P("dp"),
            P(("dp", "tensor"), None),
        ),
        out_specs=(
            P(("dp", "tensor"), None),
            P(("dp", "tensor"), None),
            P("dp", "tensor"),
            P("dp", None),
            P("dp", None),
            P("tensor", "dp"),
            P("dp"),
            P("dp"),
            P("dp"),
            P("dp"),
            P("dp", "tensor"),
            P("dp", "tensor"),
            P("tensor", "dp"),
            P("dp"),
            P("dp"),
        ),
        check_vma=False,
    )
```

profile of v0, /device:TPU:0, one launch (start us, length us, event | category | flops | bytes accessed | tf_op | source)
XLA Modules:
  0.0 1418.0 jit_solution(9678145180410714932)
XLA Ops:
  15.8 45.0 %all-reduce.14 = (bf16[640]{0:T(1024)(128)(2,1)S(1)}, bf16[256]{0:T(256)(128)(2,1)S(1)}, bf16[256]{0:T(256)(128)(2,1)S(1)}, bf16[640]{0:T(1024)(128)(2,1)S(1)}, ...) all-reduce(bf16[640]{0:T(1024)(128)(2,1)S(1)} %dynamic-update-slice, ...), channel_id=1, replica_groups=mesh['dp'=16,'tensor'=2] {'dp'}, use_global_device_ids=true, to_apply=%add | all-reduce | flops 3072 | bytes 12288
  62.5 37.6 %all_gather.61 = bf16[640,256]{1,0:T(8,128)(2,1)S(1)} all-gather(bf16[40,256]{1,0:T(8,128)(2,1)} %param.21), channel_id=1, replica_groups=mesh['dp'=16,'tensor'=2] {'dp'}, dimensions={0}, use_global_device_ids=true | all-gather | bytes 348160 | tf_op jit(solution)/shard_map/all_gather | solution.py:88
  103.3 5.1 fusion.90
  109.3 39.3 %all_gather.64 = bf16[640,256]{1,0:T(8,128)(2,1)S(1)} all-gather(bf16[40,256]{1,0:T(8,128)(2,1)S(1)} %copy-done.49), channel_id=1, replica_groups=mesh['dp'=16,'tensor'=2] {'dp'}, dimensions={0}, use_global_device_ids=true | all-gather | bytes 348160 | tf_op jit(solution)/shard_map/all_gather | solution.py:89
  150.8 42.0 %all_gather.59 = bf16[640,512]{1,0:T(8,128)(2,1)} all-gather(bf16[40,512]{1,0:T(8,128)(2,1)S(1)} %copy-done.47), channel_id=1, replica_groups=mesh['dp'=16,'tensor'=2] {'dp'}, dimensions={0}, use_global_device_ids=true | all-gather | bytes 696320 | tf_op jit(solution)/shard_map/all_gather | solution.py:87
  193.2 8.1 fusion.83
  201.3 43.3 %all_gather.66 = bf16[512,640]{0,1:T(8,128)(2,1)} all-gather(bf16[512,40]{0,1:T(8,128)(2,1)S(1)} %copy-done.48), channel_id=1, replica_groups=mesh['dp'=16,'tensor'=2] {'dp'}, dimensions={1}, use_global_device_ids=true | all-gather | bytes 696320 | tf_op jit(solution)/shard_map/all_gather | solution.py:90
  246.1 5.7 multiply_reduce_fusion.2
  251.8 5.4 copy.61
  264.7 47.1 %while.28 = (s32[]{:T(128)}, bf16[4,512,2,256]{3,2,1,0:T(2,128)(2,1)}, f32[4,2,512]{2,1,0:T(2,128)S(1)}, s32[4]{0:T(128)S(1)}, bf16[2048,2,256]{2,0,1:T(8,128)(2...) while((s32[]{:T(128)}, ...), condition=%wide.region_6.7_spmd.clone, body=%wide.region_3.6_spmd.clone.sunk | while | flops 2173959680 | bytes 37786316 | solution.py:158
  320.6 9.2 reduce-scatter.13.cloned.1.call-done
  337.1 39.4 %all-gather.18.cloned.1.call-done = bf16[640,1024]{1,0:T(8,128)(2,1)} async-done(((bf16[40,1024]{1,0:T(8,128)(2,1)}), bf16[640,1024]{1,0:T(8,128)(2,1)}) %all-gather.18.cloned.1.call-update) | async-done | bytes 1310736 | tf_op jit(solution)/shard_map/all_gather | solution.py:95
  376.4 12.2 all-gather.16.cloned.1.call-done
  388.7 8.9 fusion.98
  397.5 52.2 %all-gather.20.cloned.1.call-done = bf16[640,1024]{1,0:T(8,128)(2,1)} async-done(((bf16[40,1024]{1,0:T(8,128)(2,1)}), bf16[640,1024]{1,0:T(8,128)(2,1)}) %all-gather.20.cloned.1.call-update) | async-done | bytes 1310736 | tf_op jit(solution)/shard_map/all_gather | solution.py:96
  449.7 10.4 multiply_convert_fusion.1
  460.1 48.5 %all-gather.22.cloned.1.call-done = bf16[1024,640]{0,1:T(8,128)(2,1)} async-done(((bf16[1024,40]{0,1:T(8,128)(2,1)}), bf16[1024,640]{0,1:T(8,128)(2,1)}) %all-gather.22.cloned.1.call-update) | async-done | bytes 1310736 | tf_op jit(solution)/shard_map/all_gather | solution.py:97
  508.6 8.4 fusion.99
  517.7 11.5 reduce-scatter.15.cloned.1.call-done
  537.3 12.4 all-gather.24.cloned.1.call-done
  549.7 14.3 %multiply_convert_fusion = (bf16[2048,1024]{1,0:T(8,128)(2,1)S(1)}, bf16[2048,1024]{1,0:T(8,128)(2,1)S(1)}) fusion(f32[2048,1024]{1,0:T(8,128)} %fusion.98, f32[2048,1024]{1,0:T(8,128)} %get-tuple-element.318, bf16[2048,640]{1,0:T(8,128)(2,1)} %all-gather.24.cloned.1.call-done, bf16[1024,640]{0,1:T(8,128)(2,1)} %all-gather.22.cloned.1.call-done), kind=kOutput, calls=%fused_computation.70 | convolution fusion | flops 2734686208 | bytes 29097984 | tf_op jit(solution)/shard_map/dot_general | solution.py:17
  567.7 5.2 convolution_add_fusion
  572.9 14.5 %reduce-scatter.17.cloned.1.call-done = f32[1024,640]{1,0:T(8,128)} async-done(((f32[2048,640]{1,0:T(8,128)}), f32[1024,640]{1,0:T(8,128)}) %reduce-scatter.17.cloned.1.call-update) | async-done | bytes 2621456 | tf_op jit(solution)/shard_map/reduce_scatter | solution.py:186
  597.8 12.1 all-gather.26.cloned.1.call-done
  609.9 4.9 convolution_convert_fusion.1
  614.8 144.9 %while.29 = (s32[]{:T(128)}, f32[2048,256]{1,0:T(8,128)}, f32[2048,256]{1,0:T(8,128)}, f32[4,512,2,256]{3,1,2,0:T(8,128)}, s32[4]{0:T(128)S(1)}, /*index=5*/bf16...) while((s32[]{:T(128)}, f32[2048,256]{1,0:T(8,128)}, ...), condition=%wide.region_18.19_spmd.clone, body=%wide.region_16.18_spmd.clone.sunk | while | flops 5404098048 | bytes 127959920 | solution.py:237
  616.0 5.8 fusion.178
  624.5 6.3 fusion.179
  637.7 5.0 fusion.181
  642.6 7.4 fusion.182
  651.3 5.8 fusion.178
  659.7 6.3 fusion.179
  673.0 5.7 fusion.181
  678.7 7.9 fusion.182
  687.9 5.8 fusion.178
  696.3 6.3 fusion.179
  709.5 5.7 fusion.181
  715.2 7.9 fusion.182
  724.4 5.8 fusion.178
  732.8 6.3 fusion.179
  746.0 5.7 fusion.181
  751.7 7.9 fusion.182
  769.4 7.5 maximum_cosine_fusion
  776.9 6.1 reshape.331
  783.0 5.2 copy.72
  788.2 4.5 copy.69
  792.7 5.7 copy.67
  808.9 5.7 copy.70
  822.9 5.0 convolution_convert_fusion
  828.9 4.5 convert_multiply_fusion.4
  845.4 7.4 fusion.107
  854.6 6.7 fusion.105
  861.4 6.7 fusion.106
  868.1 5.2 fusion.102
  873.4 4.4 fusion.104
  881.9 5.0 fusion.79
  886.9 77.2 %all-reduce.12 = (f32[640]{0:T(1024)S(1)}, f32[256]{0:T(256)S(1)}, f32[256]{0:T(256)S(1)}, f32[640]{0:T(1024)S(1)}, f32[640]{0:T(1024)S(1)}, /*index=5*/f32[640]{0:T(1024)S(1)}) all-reduce(f32[640]{0:T(1024)S(1)} %get-tuple-element.232, f32[256]{0:T(256)S(1)} %get-tuple-element.224, ...), channel_id=11, replica_groups=mesh['dp'=16,'tensor'=2] {'dp'}, use_global_device_ids=true, to_apply=%region_31.32.clone | all-reduce | flops 3072 | bytes 24576
  967.6 29.9 %reduce-scatter.27.cloned.1.call-done = f32[40,256]{1,0:T(8,128)} async-done(((f32[640,256]{1,0:T(8,128)}), f32[40,256]{1,0:T(8,128)}) %reduce-scatter.27.cloned.1.call-update) | async-done | bytes 40976 | tf_op jit(solution)/shard_map/reduce_scatter | solution.py:275
  997.6 4.7 fusion.78
  1002.3 76.6 %reduce-scatter.35.cloned.1.call-done = f32[1024,40]{0,1:T(8,128)} async-done(((f32[1024,640]{0,1:T(8,128)}), f32[1024,40]{0,1:T(8,128)}) %reduce-scatter.35.cloned.1.call-update) | async-done | bytes 163856 | tf_op jit(solution)/shard_map/reduce_scatter | solution.py:198
  1078.9 82.4 %reduce-scatter.31.cloned.1.call-done = f32[40,1024]{1,0:T(8,128)} async-done(((f32[640,1024]{1,0:T(8,128)}), f32[40,1024]{1,0:T(8,128)}) %reduce-scatter.31.cloned.1.call-update) | async-done | bytes 163856 | tf_op jit(solution)/shard_map/reduce_scatter | solution.py:196
  1161.3 82.2 %reduce-scatter.33.cloned.1.call-done = f32[40,1024]{1,0:T(8,128)} async-done(((f32[640,1024]{1,0:T(8,128)}), f32[40,1024]{1,0:T(8,128)}) %reduce-scatter.33.cloned.1.call-update) | async-done | bytes 163856 | tf_op jit(solution)/shard_map/reduce_scatter | solution.py:197
  1243.5 78.7 %reduce-scatter.23.cloned.1.call-done = f32[40,512]{1,0:T(8,128)} async-done(((f32[640,512]{1,0:T(8,128)}), f32[40,512]{1,0:T(8,128)}) %reduce-scatter.23.cloned.1.call-update) | async-done | bytes 81936 | tf_op jit(solution)/shard_map/reduce_scatter | solution.py:273
  1322.2 78.1 %reduce-scatter.29.cloned.1.call-done = f32[512,40]{0,1:T(8,128)} async-done(((f32[512,640]{0,1:T(8,128)}), f32[512,40]{0,1:T(8,128)}) %reduce-scatter.29.cloned.1.call-update) | async-done | bytes 81936 | tf_op jit(solution)/shard_map/reduce_scatter | solution.py:276
  (380 shorter events, 197.8 us)
Async XLA Ops:
  8.0 92.1 %copy-start.8 = (bf16[1024,640]{1,0:T(8,128)(2,1)S(1)}, bf16[1024,640]{1,0:T(8,128)(2,1)}, u32[]{:S(2)}) copy-start(bf16[1024,640]{1,0:T(8,128)(2,1)} %param.19) | copy-start | bytes 3932164
  8.0 236.6 %all-gather.12.cloned.1.call-start = ((), (), s32[]{:S(2)}) async-start(), calls=%async_computation.13 | async-start | bytes 1572864 | tf_op jit(solution)/shard_map/all_gather | solution.py:120
  8.1 184.7 %copy-start.57 = (f32[128]{0:T(128)}, f32[128]{0:T(128)S(1)}, u32[]{:S(2)}) copy-start(f32[128]{0:T(128)S(1)} %multiply_exponential_fusion) | copy-start | bytes 1540
  60.9 39.3 %copy-start.43 = (f32[640]{0:T(1024)}, f32[640]{0:T(1024)S(1)}, u32[]{:S(2)}) copy-start(f32[640]{0:T(1024)S(1)} %convert_element_type.113) | copy-start | bytes 7684
  62.5 37.6 %copy-start.45 = (f32[1024]{0:T(1024)}, f32[1024]{0:T(1024)S(1)}, u32[]{:S(2)}) copy-start(f32[1024]{0:T(1024)S(1)} %add_rsqrt_fusion.5) | copy-start | bytes 12292
  101.2 7.2 copy-start.10
  101.2 7.2 copy-start.41
  101.2 7.2 copy-start.55
  102.5 6.8 copy-start.49
  103.3 46.0 %copy-start.15 = (bf16[1024,640]{1,0:T(8,128)(2,1)S(1)}, bf16[1024,640]{1,0:T(8,128)(2,1)}, u32[]{:S(2)}) copy-start(bf16[1024,640]{1,0:T(8,128)(2,1)} %copy-done.14) | copy-start | bytes 3932164
  108.4 42.3 %copy-start.47 = (bf16[40,512]{1,0:T(8,128)(2,1)S(1)}, bf16[40,512]{1,0:T(8,128)(2,1)}, u32[]{:S(2)}) copy-start(bf16[40,512]{1,0:T(8,128)(2,1)} %param.20) | copy-start | bytes 122884
  108.5 137.6 %all-gather.10.cloned.1.call-start = ((), (), s32[]{:S(2)}) async-start(), calls=%async_computation.12 | async-start | bytes 3932160 | tf_op jit(solution)/shard_map/all_gather | solution.py:119
  109.2 155.4 %all-gather.14.cloned.1.call-start = ((), (), s32[]{:S(2)}) async-start(), calls=%async_computation.14 | async-start | bytes 1572864 | tf_op jit(solution)/shard_map/all_gather | solution.py:121
  150.7 179.0 %reduce-scatter.13.cloned.1.call-start = ((), (), s32[]{:S(2)}) async-start(), calls=%async_computation.15 | async-start | bytes 7864320 | tf_op jit(solution)/shard_map/reduce_scatter | solution.py:160
  192.8 67.3 %copy-start.50 = (f32[256]{0:T(256)}, f32[256]{0:T(256)S(1)}, u32[]{:S(2)}) copy-start(f32[256]{0:T(256)S(1)} %convert_element_type.115) | copy-start | bytes 3076
  193.2 8.1 copy-start.48
  201.3 58.8 %copy-start.17 = (f32[2048,256]{1,0:T(8,128)}, f32[2048,256]{1,0:T(8,128)S(1)}, u32[]{:S(2)}) copy-start(f32[2048,256]{1,0:T(8,128)S(1)} %get-tuple-element.310) | copy-start | bytes 6291460
  311.8 7.9 copy-start.3
  319.7 56.7 %all-gather.18.cloned.1.call-start = ((), (), s32[]{:S(2)}) async-start(), calls=%async_computation.17 | async-start | bytes 1392640 | tf_op jit(solution)/shard_map/all_gather | solution.py:95
  320.3 68.3 %all-gather.16.cloned.1.call-start = ((), (), s32[]{:S(2)}) async-start(), calls=%async_computation.16 | async-start | bytes 3932160 | tf_op jit(solution)/shard_map/all_gather | solution.py:165
  335.7 114.0 %all-gather.20.cloned.1.call-start = ((), (), s32[]{:S(2)}) async-start(), calls=%async_computation.18 | async-start | bytes 1392640 | tf_op jit(solution)/shard_map/all_gather | solution.py:96
  336.3 172.4 %all-gather.22.cloned.1.call-start = ((), (), s32[]{:S(2)}) async-start(), calls=%async_computation.19 | async-start | bytes 1392640 | tf_op jit(solution)/shard_map/all_gather | solution.py:97
  337.0 192.2 %reduce-scatter.15.cloned.1.call-start = ((), (), s32[]{:S(2)}) async-start(), calls=%async_computation.20 | async-start | bytes 7864320 | tf_op jit(solution)/shard_map/reduce_scatter | solution.py:171
  517.0 32.7 %all-gather.24.cloned.1.call-start = ((), (), s32[]{:S(2)}) async-start(), calls=%async_computation.21 | async-start | bytes 3932160 | tf_op jit(solution)/shard_map/all_gather | solution.py:179
  537.1 50.3 %reduce-scatter.17.cloned.1.call-start = ((), (), s32[]{:S(2)}) async-start(), calls=%async_computation.22 | async-start | bytes 7864320 | tf_op jit(solution)/shard_map/reduce_scatter | solution.py:186
  549.7 14.3 %copy-start.61 = (bf16[640,1024]{1,0:T(8,128)(2,1)S(1)}, bf16[640,1024]{1,0:T(8,128)(2,1)}, u32[]{:S(2)}) copy-start(bf16[640,1024]{1,0:T(8,128)(2,1)} %all-gather.18.cloned.1.call-done) | copy-start | bytes 3932164
  572.9 37.0 %all-gather.26.cloned.1.call-start = ((), (), s32[]{:S(2)}) async-start(), calls=%async_computation.23 | async-start | bytes 3932160 | tf_op jit(solution)/shard_map/all_gather | solution.py:205
  597.3 230.7 %reduce-scatter.21.cloned.1.call-start = ((), (), s32[]{:S(2)}) async-start(), calls=%async_computation.25 | async-start | bytes 3145728 | tf_op jit(solution)/shard_map/reduce_scatter | solution.py:255
  597.8 17.0 %copy-start.4 = (bf16[2048,256]{1,0:T(8,128)(2,1)S(1)}, bf16[2048,256]{1,0:T(8,128)(2,1)}, u32[]{:S(2)}) copy-start(bf16[2048,256]{1,0:T(8,128)(2,1)} %copy-done.3) | copy-start | bytes 3145732
  616.0 8.4 copy-start.64
  624.4 6.4 slice-start
  624.5 6.4 slice-start.1
  651.3 8.4 copy-start.64
  659.7 6.4 slice-start
  659.7 6.4 slice-start.1
  687.8 8.4 copy-start.64
  696.2 6.4 slice-start
  696.3 6.4 slice-start.1
  724.4 8.4 copy-start.64
  732.8 6.4 slice-start
  732.8 6.4 slice-start.1
  766.9 114.9 %reduce-scatter.19.cloned.1.call-start = ((), (), s32[]{:S(2)}) async-start(), calls=%async_computation.24 | async-start | bytes 3932160 | tf_op jit(solution)/shard_map/reduce_scatter | solution.py:252
  769.0 7.8 copy-start.40
  792.7 5.7 copy-start.18
  808.9 10.1 copy-start.29
  814.6 4.4 copy-start.5
  814.6 4.7 copy-start.21
  827.9 5.7 copy-start.11
  827.9 5.7 copy-start.42
  827.9 5.7 copy-start.56
  827.9 139.7 %reduce-scatter.25.cloned.1.call-start = ((), (), s32[]{:S(2)}) async-start(), calls=%async_computation.27 | async-start | bytes 696320 | tf_op jit(solution)/shard_map/reduce_scatter | solution.py:274
  828.9 4.7 copy-start.31
  843.6 153.9 %reduce-scatter.27.cloned.1.call-start = ((), (), s32[]{:S(2)}) async-start(), calls=%async_computation.28 | async-start | bytes 696320 | tf_op jit(solution)/shard_map/reduce_scatter | solution.py:275
  845.1 233.7 %reduce-scatter.35.cloned.1.call-start = ((), (), s32[]{:S(2)}) async-start(), calls=%async_computation.32 | async-start | bytes 2785280 | tf_op jit(solution)/shard_map/reduce_scatter | solution.py:198
  852.9 308.4 %reduce-scatter.31.cloned.1.call-start = ((), (), s32[]{:S(2)}) async-start(), calls=%async_computation.30 | async-start | bytes 2785280 | tf_op jit(solution)/shard_map/reduce_scatter | solution.py:196
  861.3 382.1 %reduce-scatter.33.cloned.1.call-start = ((), (), s32[]{:S(2)}) async-start(), calls=%async_computation.31 | async-start | bytes 2785280 | tf_op jit(solution)/shard_map/reduce_scatter | solution.py:197
  868.1 5.4 copy-start.26
  868.1 454.1 %reduce-scatter.23.cloned.1.call-start = ((), (), s32[]{:S(2)}) async-start(), calls=%async_computation.26 | async-start | bytes 1392640 | tf_op jit(solution)/shard_map/reduce_scatter | solution.py:273
  873.4 6.3 copy-start.35
  873.4 526.9 %reduce-scatter.29.cloned.1.call-start = ((), (), s32[]{:S(2)}) async-start(), calls=%async_computation.29 | async-start | bytes 1392640 | tf_op jit(solution)/shard_map/reduce_scatter | solution.py:276
  877.9 522.4 %all-reduce.17.cloned.1.call-start = ((), (), s32[]{:S(2)}) async-start(), calls=%async_computation.33 | async-start | bytes 169984 | tf_op jit(solution)/shard_map/psum | solution.py:284
  881.8 5.0 copy-start.52
  881.8 5.0 copy-start.53
  881.9 5.0 copy-start.54
  (42 other events, 107.8 us)
Sparse Core Ops, SparseCore 0:
  108.6 6.7 all-gather.11
  116.9 12.5 all-gather.9
  150.8 5.0 all-gather.13
  319.8 9.8 reduce-scatter.12
  537.2 12.4 all-gather.23
  573.0 14.3 reduce-scatter.16
  997.7 14.6 all-reduce.16
Sparse Core Ops, SparseCore 1:
  323.0 53.4 all-gather.17
  378.5 10.1 all-gather.15
  391.7 58.0 all-gather.19
  452.9 55.7 all-gather.21
  517.1 12.1 reduce-scatter.14
  597.4 12.4 all-gather.25
  767.0 10.7 reduce-scatter.20
  828.0 11.3 reduce-scatter.18
  843.7 78.1 reduce-scatter.24
  924.2 73.3 reduce-scatter.26
  1000.4 78.4 reduce-scatter.34
  1081.8 79.4 reduce-scatter.30
  1164.1 79.3 reduce-scatter.32
  1246.4 75.7 reduce-scatter.22
  1325.1 75.1 reduce-scatter.28
where the time goes:
time: 1420 us
  waiting for transfers between devices  643 us (45%)
  blocking collectives  284 us (20%)
  matrix products  247 us (17%)
  other arithmetic  108 us (8%)
  local copies, waits for them, and re-layouts  99.6 us (7%)
  between operations  20.2 us (1%)
    unnamed x2, blocking collectives  122 us
    reduce_scatter x1, waiting for transfers between devices, per_device(): lax.psum_scatter(gate_w_grad, 'dp', scatter_dimension=0, tiled=True)  82.4 us
    reduce_scatter x1, waiting for transfers between devices, per_device(): lax.psum_scatter(up_w_grad, 'dp', scatter_dimension=0, tiled=True)  82.2 us
    reduce_scatter x1, waiting for transfers between devices, per_device(): lax.psum_scatter(query_w_grad, 'dp', scatter_dimension=0, tiled=True)  78.7 us
    reduce_scatter x1, waiting for transfers between devices, per_device(): lax.psum_scatter(out_w_grad, 'dp', scatter_dimension=1, tiled=True)  78.1 us
    reduce_scatter x1, waiting for transfers between devices, per_device(): lax.psum_scatter(down_w_grad, 'dp', scatter_dimension=1, tiled=True)  76.6 us
    all_gather x1, waiting for transfers between devices, per_device(): lax.all_gather(w_up, 'dp', axis=0, tiled=True)  52.2 us
    all_gather x1, waiting for transfers between devices, per_device(): lax.all_gather(w_down, 'dp', axis=1, tiled=True)  48.5 us
  transfers between devices with their start and end apart: 22, of which 15 were waited for; matrix products, arithmetic and copies ran while one was open for 12% of the time, Pallas kernels for 0%

commit v1 on v0

v1 whole, which is shorter than its diff:
```python
import functools
import math

import jax
import jax.numpy as jnp
from jax import lax
from jax.experimental import pallas as pl
from jax.experimental.pallas import tpu as pltpu
from jax.sharding import PartitionSpec as P

EPS = 1e-06
MASKED = -1e30


def matmul(left, right):
    return jnp.dot(left, right, preferred_element_type=jnp.float32)


def times_transposed(left, right):
    return lax.dot_general(
        left, right, (((1,), (1,)), ((), ())), preferred_element_type=jnp.float32
    )


def transposed_times(left, right):
    return lax.dot_general(
        left, right, (((0,), (0,)), ((), ())), preferred_element_type=jnp.float32
    )


def norm_rows(value, gain):
    scale = lax.rsqrt(jnp.mean(value * value, axis=-1, keepdims=True) + EPS)
    unit = value * scale
    return (unit * gain, unit, scale)


def norm_back(grad, unit, scale, gain, axes):
    gain_grad = jnp.sum(grad * unit, axis=axes)
    inner = grad * gain
    return (scale * (inner - unit * jnp.mean(inner * unit, axis=-1, keepdims=True)), gain_grad)


def tables(length, width, inner=64):
    half = width // 2
    freqs = jnp.exp(jnp.arange(half, dtype=jnp.float32) * (-2.0 * math.log(1000000.0) / width))
    coarse = (jnp.arange(length // inner, dtype=jnp.float32) * inner)[:, None] * freqs
    fine = jnp.arange(inner, dtype=jnp.float32)[:, None] * freqs
    cos_a, sin_a = jnp.cos(coarse)[:, None], jnp.sin(coarse)[:, None]
    cos_b, sin_b = jnp.cos(fine)[None], jnp.sin(fine)[None]
    cosine = (cos_a * cos_b - sin_a * sin_b).reshape(length, half)
    sine = (sin_a * cos_b + cos_a * sin_b).reshape(length, half)
    return cosine, sine


def turn(value, cosine, sine):
    half = value.shape[-1] // 2
    first, second = value[:, :half], value[:, half:]
    return jnp.concatenate(
        [first * cosine - second * sine, second * cosine + first * sine], axis=-1
    )


def turn_back(grad, cosine, sine):
    half = grad.shape[-1] // 2
    first, second = grad[:, :half], grad[:, half:]
    return jnp.concatenate(
        [first * cosine + second * sine, second * cosine - first * sine], axis=-1
    )


def gelu_tanh(value):
    return jax.nn.gelu(value, approximate=True)


BLOCK = 512
VMEM = 56 * 1024 * 1024


def allowed_keys(size):
    keys = lax.broadcasted_iota(jnp.int32, (size, size), 0)
    queries = lax.broadcasted_iota(jnp.int32, (size, size), 1)
    return queries >= keys


def attend_kernel(heads, width, factor, q_ref, k_ref, vt_ref, o_ref, lse_ref, acc, peak, total):
    block = q_ref.shape[0]
    number = pl.program_id(0)
    queries = [q_ref[:, h * width : (h + 1) * width] * jnp.bfloat16(factor) for h in range(heads)]

    def tile(j, first):
        start = pl.multiple_of(j * block, block)
        keys = k_ref[pl.ds(start, block), :]
        values = vt_ref[:, pl.ds(start, block)]
        for h in range(heads):
            scores = times_transposed(keys, queries[h])
            if first:
                scores = jnp.where(allowed_keys(block), scores, MASKED)
                top = jnp.max(scores, axis=0, keepdims=True)
                expon = jnp.exp(scores - top)
                total[h] = jnp.sum(expon, axis=0, keepdims=True)
                acc[h] = matmul(values, expon.astype(jnp.bfloat16))
            else:
                old = peak[h]
                top = jnp.maximum(old, jnp.max(scores, axis=0, keepdims=True))
                expon = jnp.exp(scores - top)
                scale = jnp.exp(old - top)
                total[h] = total[h] * scale + jnp.sum(expon, axis=0, keepdims=True)
                acc[h] = acc[h] * scale + matmul(values, expon.astype(jnp.bfloat16))
            peak[h] = top

    tile(number, True)

    @pl.loop(0, number)
    def _(j):
        tile(j, False)

    for h in range(heads):
        mixed = acc[h] * (1.0 / total[h])
        o_ref[:, h * width : (h + 1) * width] = mixed.T.astype(jnp.bfloat16)
        lse_ref[h] = peak[h] + jnp.log(total[h])


def attend(query, key, value_t, heads):
    length, width = key.shape
    block = min(BLOCK, length)
    return pl.pallas_call(
        functools.partial(attend_kernel, heads, width, width ** (-0.5)),
        grid=(length // block,),
        in_specs=[
            pl.BlockSpec((block, heads * width), lambda i: (i, 0)),
            pl.BlockSpec((length, width), lambda i: (0, 0)),
            pl.BlockSpec((width, length), lambda i: (0, 0)),
        ],
        out_specs=[
            pl.BlockSpec((block, heads * width), lambda i: (i, 0)),
            pl.BlockSpec((heads, 1, block), lambda i: (0, 0, i)),
        ],
        out_shape=[
            jax.ShapeDtypeStruct((length, heads * width), jnp.bfloat16),
            jax.ShapeDtypeStruct((heads, 1, length), jnp.float32),
        ],
        scratch_shapes=[
            pltpu.VMEM((heads, width, block), jnp.float32),
            pltpu.VMEM((heads, 1, block), jnp.float32),
            pltpu.VMEM((heads, 1, block), jnp.float32),
        ],
        compiler_params=pltpu.CompilerParams(vmem_limit_bytes=VMEM),
        cost_estimate=pl.CostEstimate(
            flops=4 * heads * length * length * width,
            bytes_accessed=8 * length * heads * width,
            transcendentals=heads * length * length,
        ),
        name="attend",
    )(query, key, value_t)


def attend_back_kernel(
    heads, width, factor, q_ref, g_ref, o_ref, lse_ref, k_ref, kt_ref, v_ref,
    dq_ref, dk_ref, dv_ref, dqt, delta,
):
    block = q_ref.shape[0]
    number = pl.program_id(0)
    cols = [slice(h * width, (h + 1) * width) for h in range(heads)]
    queries = [q_ref[:, c] * jnp.bfloat16(factor) for c in cols]

    @pl.when(number == 0)
    def _():
        dk_ref[...] = jnp.zeros_like(dk_ref)
        dv_ref[...] = jnp.zeros_like(dv_ref)

    for h in range(heads):
        product = g_ref[:, cols[h]].astype(jnp.float32) * o_ref[:, cols[h]].astype(jnp.float32)
        delta[h] = jnp.sum(product.T, axis=0, keepdims=True)

    def tile(j, first):
        start = pl.multiple_of(j * block, block)
        rows = pl.ds(start, block)
        keys = k_ref[rows, :]
        keys_t = kt_ref[:, rows]
        values = v_ref[rows, :]
        key_grad = value_grad = None
        for h in range(heads):
            grads = g_ref[:, cols[h]]
            scores = times_transposed(keys, queries[h])
            prob = jnp.exp(scores - lse_ref[h])
            if first:
                prob = jnp.where(allowed_keys(block), prob, 0.0)
            prob_grad = times_transposed(values, grads)
            score_grad = (prob * (prob_grad - delta[h])).astype(jnp.bfloat16)
            more_value = matmul(prob.astype(jnp.bfloat16), grads)
            more_key = matmul(score_grad, queries[h])
            value_grad = more_value if value_grad is None else value_grad + more_value
            key_grad = more_key if key_grad is None else key_grad + more_key
            if first:
                dqt[h] = matmul(keys_t, score_grad)
            else:
                dqt[h] += matmul(keys_t, score_grad)
        dk_ref[rows, :] += key_grad
        dv_ref[rows, :] += value_grad

    tile(number, True)

    @pl.loop(0, number)
    def _(j):
        tile(j, False)

    for h in range(heads):
        dq_ref[:, cols[h]] = dqt[h].T * factor


def attend_back(query, grad, mixed, lse, key, key_t, value, heads):
    length, width = key.shape
    block = min(BLOCK, length)
    rows = pl.BlockSpec((block, heads * width), lambda i: (i, 0))
    whole = pl.BlockSpec((length, width), lambda i: (0, 0))
    return pl.pallas_call(
        functools.partial(attend_back_kernel, heads, width, width ** (-0.5)),
        grid=(length // block,),
        in_specs=[
            rows,
            rows,
            rows,
            pl.BlockSpec((heads, 1, block), lambda i: (0, 0, i)),
            whole,
            pl.BlockSpec((width, length), lambda i: (0, 0)),
            whole,
        ],
        out_specs=[rows, whole, whole],
        out_shape=[
            jax.ShapeDtypeStruct((length, heads * width), jnp.float32),
            jax.ShapeDtypeStruct((length, width), jnp.float32),
            jax.ShapeDtypeStruct((length, width), jnp.float32),
        ],
        scratch_shapes=[
            pltpu.VMEM((heads, width, block), jnp.float32),
            pltpu.VMEM((heads, 1, block), jnp.float32),
        ],
        compiler_params=pltpu.CompilerParams(vmem_limit_bytes=VMEM),
        cost_estimate=pl.CostEstimate(
            flops=10 * heads * length * length * width,
            bytes_accessed=12 * length * heads * width,
            transcendentals=heads * length * length,
        ),
        name="attend_back",
    )(query, grad, mixed, lse, key, key_t, value)


def per_device(
    tokens,
    w_query,
    w_key,
    w_value,
    w_out,
    gain_attn,
    gain_query,
    gain_key,
    gain_post_attn,
    w_gate,
    w_up,
    w_down,
    gain_pre_ffn,
    gain_post_ffn,
    cotangent,
):
    parts = lax.axis_size("tensor")
    spread = lax.axis_size("dp")
    own_rows = tokens.shape[0]
    length = own_rows * parts
    head_dim = w_key.shape[1]
    model = w_query.shape[0] * spread
    share = w_query.shape[0]
    small = gain_query.shape[0]
    heads = w_query.shape[1] // head_dim
    offset = lax.axis_index("tensor") * own_rows
    swap = [(i, (i + 1) % parts) for i in range(parts)]

    def whole_sequence(rows):
        pieces = [rows]
        for _ in range(parts - 1):
            pieces.append(lax.ppermute(pieces[-1], "tensor", swap))
        if parts == 1:
            return rows
        first = lax.axis_index("tensor") == 0
        return jnp.concatenate(
            [jnp.where(first, pieces[0], pieces[1]), jnp.where(first, pieces[1], pieces[0])], axis=0
        )

    def summed(partial):
        low = partial.astype(jnp.bfloat16)
        return low.astype(jnp.float32) + lax.ppermute(low, "tensor", swap).astype(jnp.float32)

    def own(rows):
        return lax.dynamic_slice_in_dim(rows, offset, own_rows, 0)

    def tall(column):
        return jnp.pad(column, (0, share - small))

    gain_block = jnp.stack(
        [gain_attn, gain_post_attn, gain_pre_ffn, gain_post_ffn, tall(gain_query), tall(gain_key)],
        axis=1,
    )
    gain_block = jnp.pad(gain_block, ((0, 0), (0, 128 - gain_block.shape[1])))
    attn_pack = jnp.concatenate([w_query, w_key, w_value, w_out.T, gain_block], axis=1)
    ffn_pack = jnp.concatenate([w_gate, w_up, w_down.T], axis=1)
    attn_all = lax.all_gather(attn_pack, "dp", axis=0, tiled=True)
    attn_all, ffn_pack = lax.optimization_barrier((attn_all, ffn_pack))
    ffn_all = lax.all_gather(ffn_pack, "dp", axis=0, tiled=True)
    low_tokens = whole_sequence(tokens)
    inputs = low_tokens.astype(jnp.float32)
    out_grad = whole_sequence(cotangent).astype(jnp.float32)

    q_cols = heads * head_dim
    places = [0, q_cols, q_cols + head_dim, q_cols + 2 * head_dim, 2 * q_cols + 2 * head_dim]
    query_w, key_w, value_w, out_wt = (
        attn_all[:, places[n] : places[n + 1]] for n in range(4)
    )
    gains = attn_all[:, places[4] :].astype(jnp.float32)
    attn_g, post_attn_g, pre_ffn_g, post_ffn_g = (gains[:, n] for n in range(4))
    query_g, key_g = (
        gains[:, n].reshape(spread, share)[:, :small].reshape(spread * small) for n in (4, 5)
    )
    hidden_units = w_gate.shape[1]
    gate_w, up_w, down_wt = (
        ffn_all[:, n * hidden_units : (n + 1) * hidden_units] for n in range(3)
    )
    cosine, sine = tables(length, head_dim)

    normed, attn_unit, attn_scale = norm_rows(inputs, attn_g)
    normed_low = normed.astype(jnp.bfloat16)
    key_pre = matmul(normed_low, key_w)
    value_low = matmul(normed_low, value_w).astype(jnp.bfloat16)
    key_normed, key_unit, key_scale = norm_rows(key_pre, key_g)
    key_low = turn(key_normed, cosine, sine).astype(jnp.bfloat16)
    query_pre = matmul(normed_low, query_w)
    query_units, query_scales, query_lows = [], [], []
    for h in range(heads):
        normal, unit, scale = norm_rows(query_pre[:, h * head_dim : (h + 1) * head_dim], query_g)
        query_units.append(unit)
        query_scales.append(scale)
        query_lows.append(turn(normal, cosine, sine).astype(jnp.bfloat16))
    query_low = jnp.concatenate(query_lows, axis=1)
    mixed, lse = attend(query_low, key_low, value_low.T, heads)

    attn_sum = summed(times_transposed(mixed, out_wt))
    attn_branch, post_attn_unit, post_attn_scale = norm_rows(attn_sum, post_attn_g)
    middle = inputs + attn_branch
    ffn_normed, pre_ffn_unit, pre_ffn_scale = norm_rows(middle, pre_ffn_g)
    ffn_low = ffn_normed.astype(jnp.bfloat16)
    gate = matmul(ffn_low, gate_w)
    up = matmul(ffn_low, up_w)
    activated, gelu_pull = jax.vjp(gelu_tanh, gate)
    hidden = (activated * up).astype(jnp.bfloat16)
    ffn_sum = summed(times_transposed(hidden, down_wt))
    ffn_branch, post_ffn_unit, post_ffn_scale = norm_rows(ffn_sum, post_ffn_g)
    output = own((middle + ffn_branch).astype(jnp.bfloat16))

    ffn_sum_grad, post_ffn_gain_grad = norm_back(
        out_grad, post_ffn_unit, post_ffn_scale, post_ffn_g, 0
    )
    ffn_sum_low = ffn_sum_grad.astype(jnp.bfloat16)
    hidden_grad = matmul(ffn_sum_low, down_wt)
    gate_grad = gelu_pull(hidden_grad * up)[0].astype(jnp.bfloat16)
    up_grad = (hidden_grad * activated).astype(jnp.bfloat16)
    ffn_in_part = times_transposed(gate_grad, gate_w) + times_transposed(up_grad, up_w)
    ffn_in_grad = summed(ffn_in_part)
    ffn_grads = jnp.concatenate(
        [
            transposed_times(ffn_low, gate_grad),
            transposed_times(ffn_low, up_grad),
            transposed_times(ffn_sum_low, hidden),
        ],
        axis=1,
    )
    middle_part, pre_ffn_gain_grad = norm_back(
        ffn_in_grad, pre_ffn_unit, pre_ffn_scale, pre_ffn_g, 0
    )
    middle_grad = out_grad + middle_part
    attn_sum_grad, post_attn_gain_grad = norm_back(
        middle_grad, post_attn_unit, post_attn_scale, post_attn_g, 0
    )
    attn_sum_low = attn_sum_grad.astype(jnp.bfloat16)
    ffn_grads, attn_sum_low = lax.optimization_barrier((ffn_grads, attn_sum_low))
    ffn_owned = lax.psum_scatter(ffn_grads, "dp", scatter_dimension=0, tiled=True)

    mixed_grad = matmul(attn_sum_low, out_wt).astype(jnp.bfloat16)
    out_wt_grad = transposed_times(attn_sum_low, mixed)
    query_grad, key_grad, value_grad = attend_back(
        query_low, mixed_grad, mixed, lse, key_low, key_low.T, value_low, heads
    )
    query_gain_grad = 0.0
    query_pre_grads = []
    for h in range(heads):
        turned = turn_back(query_grad[:, h * head_dim : (h + 1) * head_dim], cosine, sine)
        pre_grad, gain_grad = norm_back(turned, query_units[h], query_scales[h], query_g, 0)
        query_pre_grads.append(pre_grad.astype(jnp.bfloat16))
        query_gain_grad = query_gain_grad + gain_grad
    key_turned = turn_back(key_grad, cosine, sine)
    key_pre_grad, key_gain_grad = norm_back(key_turned, key_unit, key_scale, key_g, 0)
    joint_grad = jnp.concatenate(
        query_pre_grads + [key_pre_grad.astype(jnp.bfloat16), value_grad.astype(jnp.bfloat16)],
        axis=1,
    )
    normed_part = times_transposed(joint_grad, attn_all[:, : places[3]])
    joint_w_grad = transposed_times(normed_low, joint_grad)
    attn_gain_grad = jnp.sum(normed_part * attn_unit, axis=0)

    def wide(column):
        return jnp.pad(column.reshape(spread, small), ((0, 0), (0, share - small))).reshape(model)

    once = 1.0 / parts
    gain_grads = jnp.stack(
        [
            attn_gain_grad,
            post_attn_gain_grad * once,
            pre_ffn_gain_grad * once,
            post_ffn_gain_grad * once,
            wide(query_gain_grad),
            wide(key_gain_grad),
        ],
        axis=1,
    )
    gain_grads = jnp.pad(gain_grads, ((0, 0), (0, 512 - gain_grads.shape[1])))
    attn_owned = lax.psum_scatter(
        jnp.concatenate([joint_w_grad, out_wt_grad, gain_grads], axis=1),
        "dp",
        scatter_dimension=0,
        tiled=True,
    )
    normed_low_part = normed_part.astype(jnp.bfloat16)
    theirs = lax.dynamic_slice_in_dim(
        normed_low_part, (length - own_rows) - offset, own_rows, 0
    )
    normed_grad = own(normed_part) + lax.ppermute(theirs, "tensor", swap).astype(jnp.float32)
    input_part, _ = norm_back(normed_grad, own(attn_unit), own(attn_scale), attn_g, 0)
    tokens_grad = own(middle_grad) + input_part

    shared = lax.psum(
        jnp.concatenate([attn_owned[:, q_cols : places[3]], attn_owned[:, places[4] : places[4] + 128]], axis=1),
        "tensor",
    )
    gain_owned = shared[:, 2 * head_dim :]
    return (
        output,
        tokens_grad,
        attn_owned[:, :q_cols],
        shared[:, :head_dim],
        shared[:, head_dim : 2 * head_dim],
        attn_owned[:, places[3] : places[4]].T,
        gain_owned[:, 0],
        gain_owned[:small, 4],
        gain_owned[:small, 5],
        gain_owned[:, 1],
        ffn_owned[:, :hidden_units],
        ffn_owned[:, hidden_units : 2 * hidden_units],
        ffn_owned[:, 2 * hidden_units :].T,
        gain_owned[:, 2],
        gain_owned[:, 3],
    )


def solution(mesh):
    return jax.shard_map(
        per_device,
        mesh=mesh,
        in_specs=(
            P(("dp", "tensor"), None),
            P("dp", "tensor"),
            P("dp", None),
            P("dp", None),
            P("tensor", "dp"),
            P("dp"),
            P("dp"),
            P("dp"),
            P("dp"),
            P("dp", "tensor"),
            P("dp", "tensor"),
            P("tensor", "dp"),
            P("dp"),
            P("dp"),
            P(("dp", "tensor"), None),
        ),
        out_specs=(
            P(("dp", "tensor"), None),
            P(("dp", "tensor"), None),
            P("dp", "tensor"),
            P("dp", None),
            P("dp", None),
            P("tensor", "dp"),
            P("dp"),
            P("dp"),
            P("dp"),
            P("dp"),
            P("dp", "tensor"),
            P("dp", "tensor"),
            P("tensor", "dp"),
            P("dp"),
            P("dp"),
        ),
        check_vma=False,
    )
```

time: 1420 us -> 634 us (0.45)
  waiting for transfers between devices: 643 us -> 357 us
  blocking collectives: 284 us -> 0 us
  matrix products: 247 us -> 80.2 us
  local copies, waits for them, and re-layouts: 99.6 us -> 59.7 us
  Pallas kernels: 0 us -> 39.4 us
  other arithmetic: 108 us -> 72.8 us
    reduce_scatter x12 -> x2, waiting for transfers between devices: 463 us -> 272 us  [the longest x1 158 us: per_device(): lax.psum_scatter(ffn_grads, 'dp', scatter_dimension=0, tiled=True)]
    all_gather x4 -> x0, blocking collectives: 162 us -> none  [the longest x1 43.3 us: per_device(): lax.all_gather(w_out, 'dp', axis=1, tiled=True)]
    dot_general x28 -> x0, matrix products: 134 us -> none  [the longest x8 35.2 us: scores_of(): jnp.einsum('qhd,kd->hqk', query_block, key_full, preferred_element_type=j...]
    unnamed x2 -> x0, blocking collectives: 122 us -> none
    all_gather x9 -> x2, waiting for transfers between devices: 177 us -> 74.6 us  [the longest x1 53.8 us: per_device(): attn_all = lax.all_gather(attn_pack, 'dp', axis=0, tiled=True)]
    pallas_call x0 -> x2, Pallas kernels: none -> 39.4 us  [the longest x1 23.3 us: attend_back(): pl.pallas_call(functools.partial(attend_back_kernel, heads, width, width...]
    while x44 -> x0, local copies, waits for them, and re-layouts: 22.7 us -> none  [the longest x4 14.5 us: per_device(): lax.scan(backward_block, (zeros, zeros), jnp.arange(blocks, dtype=jnp.int...]
    unnamed x162 -> x121, local copies, waits for them, and re-layouts: 44.4 us -> 23.9 us
  transfers between devices with their start and end apart: 22 -> 11, of which waited for: 15 -> 7; matrix products, arithmetic and copies ran while one was open for 12% -> 11% of each run, Pallas kernels for 0% -> 3%
where the time goes in v1:
time: 634 us; the launch traced here: 626 us
  waiting for transfers between devices  357 us (56%)
  matrix products  80.2 us (13%)
  other arithmetic  72.8 us (11%)
  local copies, waits for them, and re-layouts  59.7 us (9%)
  Pallas kernels  39.4 us (6%)
  between operations  15.2 us (2%)
    reduce_scatter x1, waiting for transfers between devices, per_device(): lax.psum_scatter(ffn_grads, 'dp', scatter_dimension=0, tiled=True)  158 us
    reduce_scatter x1, waiting for transfers between devices, per_device(): lax.psum_scatter(jnp.concatenate([joint_w_grad, out_wt_grad, gain_grads],...  114 us
    all_gather x1, waiting for transfers between devices, per_device(): attn_all = lax.all_gather(attn_pack, 'dp', axis=0, tiled=True)  53.8 us
    dot_general x7, matrix products, matmul(): return jnp.dot(left, right, preferred_element_type=jnp.float32)  42.1 us
    unnamed x121, local copies, waits for them, and re-layouts  23.9 us
    pallas_call x1, Pallas kernels, attend_back(): pl.pallas_call(functools.partial(attend_back_kernel, heads, width, width...  23.3 us
    dot_general x5, matrix products, times_transposed(): lax.dot_general(left, right, (((1,), (1,)), ((), ())), preferred_element_...  22.6 us
    all_gather x1, waiting for transfers between devices, per_device(): ffn_all = lax.all_gather(ffn_pack, 'dp', axis=0, tiled=True)  20.8 us
  transfers between devices with their start and end apart: 11, of which 7 were waited for; matrix products, arithmetic and copies ran while one was open for 11% of the time, Pallas kernels for 3%

profile of v1, /device:TPU:0, one launch (start us, length us, event | category | flops | bytes accessed | tf_op | source)
XLA Modules:
  0.0 626.0 jit_solution(8354850517993474116)
XLA Ops:
  12.5 1.6 copy.115
  17.9 1.6 pad_maximum_fusion.11
  19.5 1.5 broadcast_select_fusion.3
  22.6 53.8 %all-gather.3.cloned.1.call-done = bf16[640,1664]{1,0:T(8,128)(2,1)} async-done(((bf16[40,1664]{1,0:T(8,128)(2,1)}), bf16[640,1664]{1,0:T(8,128)(2,1)}) %all-gather.3.cloned.1.call-update) | async-done | bytes 2129936 | tf_op jit(solution)/shard_map/all_gather | solution.py:305
  78.4 2.6 multiply_reduce_fusion.15
  81.0 5.6 fusion.33
  87.0 2.6 multiply_reduce_fusion.17
  90.0 1.9 copy-done.1
  93.5 2.2 subtract_convert_fusion
  95.8 2.7 copy.130.q_ref
  98.5 2.9 fusion.44
  101.4 2.3 copy.131.k_ref
  103.7 3.2 convolution_convert_fusion.3.v_ref
  106.9 2.3 copy.132.vt_ref
  109.2 16.1 %attend.1 = (bf16[2048,512]{1,0:T(8,128)(2,1)}, f32[2,1,2048]{2,1,0:T(1,128)}) custom-call(bf16[2048,512]{1,0:T(8,128)(2,1)} %copy.130.q_ref, bf16[2048,256]{1,0:T(8,128)(2,1)} %copy.131.k_ref, bf16[256,2048]{1,0:T(8,128)(2,1)} %copy.132.vt_ref), custom_call_target="tpu_custom_call" | custom-call | flops 8589934592 | bytes 8388608 | tf_op jit(solution)/shard_map/attend/pallas_call | solution.py:126
  125.3 3.3 convolution_convert_fusion
  128.7 4.9 collective-permute-done.1
  135.1 2.0 multiply_reduce_fusion.6
  137.2 2.3 copy-done
  139.4 2.0 multiply_convert_fusion.3
  141.4 20.8 %all-gather.5.cloned.1.call-done = bf16[640,3072]{1,0:T(8,128)(2,1)} async-done(((bf16[40,3072]{1,0:T(8,128)(2,1)}), bf16[640,3072]{1,0:T(8,128)(2,1)}) %all-gather.5.cloned.1.call-update) | async-done | bytes 3932176 | tf_op jit(solution)/shard_map/all_gather | solution.py:307
  162.2 5.8 fusion.30
  168.0 8.2 %multiply_convert_fusion.1 = (bf16[2048,1024]{1,0:T(8,128)(2,1)S(1)}, f32[2048,1024]{1,0:T(8,128)}) fusion(f32[2048,1024]{1,0:T(8,128)S(1)} %fusion.30, bf16[2048,640]{0,1:T(8,128)(2,1)S(1)} %copy-done.26, bf16[640,3072]{1,0:T(8,128)(2,1)S(1)} %copy-done.46), kind=kOutput, calls=%fused_computation.10 | convolution fusion | flops 2705326080 | bytes 24903680 | tf_op jit(solution)/shard_map/dot_general | solution.py:16
  176.3 4.2 convolution_convert_fusion.1
  180.5 2.5 copy.134
  183.5 4.0 collective-permute-done.3
  187.5 1.5 broadcast_select_fusion.1
  189.0 4.6 multiply_reduce_fusion.5
  193.6 4.6 fusion.13
  198.2 1.4 fusion.11
  202.2 12.3 %multiply_convert_fusion = (bf16[2048,1024]{1,0:T(8,128)(2,1)}, bf16[2048,1024]{1,0:T(8,128)(2,1)}) fusion(f32[2048,1024]{1,0:T(8,128)S(1)} %bitcast.49, f32[2048,1024]{1,0:T(8,128)} %get-tuple-element.159, bf16[2048,640]{0,1:T(8,128)(2,1)S(1)} %fusion.11, bf16[640,3072]{1,0:T(8,128)(2,1)S(1)} %copy-done.47), kind=kOutput, calls=%fused_computation.9 | convolution fusion | flops 2734686208 | bytes 29097984 | tf_op jit(solution)/shard_map/dot_general | solution.py:16
  214.5 4.9 fusion.28
  219.4 4.4 add_convert_fusion
  224.0 2.9 fusion.49
  226.9 2.9 fusion.48
  229.8 2.9 fusion.47
  232.7 3.5 pad_maximum_fusion
  236.3 5.9 multiply_reduce_fusion
  242.2 7.4 %multiply_reduce_fusion.1 = (f32[640]{0:T(1024)S(1)}, f32[2048]{0:T(1024)S(1)}, f32[2048,640]{0,1:T(8,128)S(1)}) fusion(bf16[2048,640]{0,1:T(8,128)(2,1)S(1)} %copy-done.4, bf16[2048,640]{0,1:T(8,128)(2,1)S(1)} %convolution_convert_fusion, f32[2048]{0:T(1024)S(1)} %add_rsqrt_fusion.2, f32[640]{0:T(1024)S(1)} %get-tuple-element.96, ...), kind=kLoop, calls=%fused_computation.29 | loop fusion | flops 28833152 | bytes 23633408 | tf_op jit(solution)/shard_map/reduce_sum | solution.py:38
  249.6 1.9 multiply_convert_fusion.2
  251.9 4.4 convolution_convert_fusion.2.g_ref
  256.4 2.6 fusion.50
  259.0 23.3 %attend_back.1 = (f32[2048,512]{1,0:T(8,128)}, f32[2048,256]{1,0:T(8,128)}, f32[2048,256]{1,0:T(8,128)}) custom-call(bf16[2048,512]{1,0:T(8,128)(2,1)} %copy.130.q_ref, bf16[2048,512]{1,0:T(8,128)(2,1)} %convolution_convert_fusion.2.g_ref, bf16[2048,512]{1,0:T(8,128)(2,1)} %get-tuple-element.25.o_ref, f32[2,1,2048]{2,1,0:T(1,128)} %get-tuple-element.28.lse_ref, ...), custom_call_target="tpu_custom_call" | custom-call | flops 21474836480 | bytes 12582912 | tf_op jit(solution)/shard_map/attend_back/pallas_call | solution.py:216
  282.3 1.8 copy.158
  284.1 5.8 copy.140
  289.9 3.3 copy.152
  293.2 3.9 multiply_add_fusion.3
  298.5 1.6 copy-done.2
  303.8 5.8 multiply_reduce_fusion.2
  309.6 4.2 fusion.32
  314.4 4.1 select_maximum_fusion
  318.6 114.2 %reduce-scatter.3.cloned.1.call-done = f32[40,2048]{1,0:T(8,128)} async-done(((f32[640,2048]{1,0:T(8,128)}), f32[40,2048]{1,0:T(8,128)}) %reduce-scatter.3.cloned.1.call-update) | async-done | bytes 327696 | tf_op jit(solution)/shard_map/reduce_scatter | solution.py:423
  432.8 1.6 slice_bitcast_fusion.1
  436.4 3.0 dynamic-slice_convert_fusion
  439.4 2.8 fusion.17
  442.3 1.4 copy.164
  443.7 3.5 multiply_reduce_fusion.8
  447.2 4.3 multiply_add_fusion
  451.6 2.1 copy.165
  454.8 1.5 slice_reduce_fusion.10
  456.2 1.7 slice_reduce_fusion.6
  457.9 1.4 fusion.46
  459.3 157.8 %reduce-scatter.5.cloned.1.call-done = f32[40,3072]{1,0:T(8,128)} async-done(((f32[640,3072]{1,0:T(8,128)}), f32[40,3072]{1,0:T(8,128)}) %reduce-scatter.5.cloned.1.call-update) | async-done | bytes 491536 | tf_op jit(solution)/shard_map/reduce_scatter | solution.py:383
  617.2 1.9 slice_bitcast_fusion
  (195 shorter events, 28.9 us)
Async XLA Ops:
  7.2 69.2 %all-gather.3.cloned.1.call-start = ((), (), s32[]{:S(2)}) async-start(), calls=%async_computation.2 | async-start | bytes 2263040 | tf_op jit(solution)/shard_map/all_gather | solution.py:305
  12.5 149.7 %all-gather.5.cloned.1.call-start = ((), (), s32[]{:S(2)}) async-start(), calls=%async_computation.3 | async-start | bytes 4177920 | tf_op jit(solution)/shard_map/all_gather | solution.py:307
  14.1 5.4 collective-permute-start
  15.3 2.6 copy-start.36
  21.0 82.7 %copy-start.13 = (bf16[1024,640]{0,1:T(8,128)(2,1)}, bf16[1024,640]{0,1:T(8,128)(2,1)S(1)}, u32[]{:S(2)}) copy-start(bf16[1024,640]{0,1:T(8,128)(2,1)S(1)} %get-tuple-element.132) | copy-start | bytes 3932164
  22.6 81.1 %copy-start.39 = (f32[2048]{0:T(1024)}, f32[2048]{0:T(1024)S(1)}, u32[]{:S(2)}) copy-start(f32[2048]{0:T(1024)S(1)} %add_rsqrt_fusion.6) | copy-start | bytes 24580
  78.4 25.3 %copy-start.37 = (f32[640]{0:T(1024)}, f32[640]{0:T(1024)S(1)}, u32[]{:S(2)}) copy-start(f32[640]{0:T(1024)S(1)} %get-tuple-element.99) | copy-start | bytes 7684
  78.4 2.6 copy-start.17
  81.0 8.7 %copy-start.11 = (f32[2048,256]{0,1:T(8,128)}, f32[2048,256]{0,1:T(8,128)S(1)}, u32[]{:S(2)}) copy-start(f32[2048,256]{0,1:T(8,128)S(1)} %get-tuple-element.157) | copy-start | bytes 6291460
  86.8 3.2 copy-start.43
  86.8 3.2 copy-start.30
  87.0 3.0 copy-start.41
  89.6 2.9 copy-start.32
  89.7 2.9 copy-start.34
  89.7 343.1 %reduce-scatter.3.cloned.1.call-start = ((), (), s32[]{:S(2)}) async-start(), calls=%async_computation.4 | async-start | bytes 5570560 | tf_op jit(solution)/shard_map/reduce_scatter | solution.py:423
  89.7 2.2 copy-start.1
  91.9 1.5 copy-start.23
  98.5 5.2 copy-start.18
  128.6 6.5 %copy-start.14 = (bf16[1024,640]{0,1:T(8,128)(2,1)S(1)}, bf16[1024,640]{0,1:T(8,128)(2,1)}, u32[]{:S(2)}) copy-start(bf16[1024,640]{0,1:T(8,128)(2,1)} %copy-done.13) | copy-start | bytes 3932164
  128.6 6.5 %copy-start.19 = (bf16[1024,640]{0,1:T(8,128)(2,1)S(1)}, bf16[1024,640]{0,1:T(8,128)(2,1)}, u32[]{:S(2)}) copy-start(bf16[1024,640]{0,1:T(8,128)(2,1)} %copy-done.16) | copy-start | bytes 3932164
  128.6 5.0 collective-permute-start.1
  133.6 1.5 copy-start.3
  137.1 2.3 copy-start
  162.2 5.8 copy-start.26
  162.2 5.8 copy-start.46
  168.0 8.2 %copy-start.48 = (f32[2048,1024]{1,0:T(8,128)}, f32[2048,1024]{1,0:T(8,128)S(1)}, u32[]{:S(2)}) copy-start(f32[2048,1024]{1,0:T(8,128)S(1)} %fusion.30) | copy-start | bytes 25165828
  176.3 4.2 copy-start.51
  180.5 8.5 %collective-permute-start.2 = (bf16[2048,640]{0,1:T(8,128)(2,1)}, bf16[2048,640]{0,1:T(8,128)(2,1)}, u32[]{:S(2)}, u32[]{:S(2)}) collective-permute-start(bf16[2048,640]{0,1:T(8,128)(2,1)} %convolution_convert_fusion.1), channel_id=1, source_target_pairs={{0,1},{1,0},{2,3},{3,2},{4,5},{5,4},{6,7},{7,6},{8,9},{9,8},{10,11... | collective-permute-start | bytes 7864328 | tf_op jit(solution)/shard_map/ppermute | solution.py:290
  182.9 4.5 collective-permute-start.3
  189.0 9.2 %copy-start.7 = (bf16[1024,640]{0,1:T(8,128)(2,1)}, bf16[1024,640]{0,1:T(8,128)(2,1)S(1)}, u32[]{:S(2)}) copy-start(bf16[1024,640]{0,1:T(8,128)(2,1)S(1)} %get-tuple-element.130) | copy-start | bytes 3932164
  189.0 9.2 %copy-start.9 = (bf16[1024,640]{0,1:T(8,128)(2,1)}, bf16[1024,640]{0,1:T(8,128)(2,1)S(1)}, u32[]{:S(2)}) copy-start(bf16[1024,640]{0,1:T(8,128)(2,1)S(1)} %get-tuple-element.131) | copy-start | bytes 3932164
  189.0 11.9 %slice-start = ((s8[8388608]{0:T(1024)(128)(4,1)}), s8[4194304]{0:T(1024)(128)(4,1)S(1)}, s32[]{:S(2)}) async-start(s8[8388608]{0:T(1024)(128)(4,1)} %bitcast.48), calls=%async_computation.8 | async-start | bytes 8388608
  193.6 7.3 %slice-start.1 = ((s8[8388608]{0:T(1024)(128)(4,1)}), s8[4194304]{0:T(1024)(128)(4,1)S(1)}, s32[]{:S(2)}) async-start(s8[8388608]{0:T(1024)(128)(4,1)} %bitcast.48), calls=%async_computation.9 | async-start | bytes 8388608
  198.2 2.7 copy-start.5
  198.2 4.0 copy-start.47
  214.5 4.9 copy-start.53
  219.4 4.6 copy-start.52
  223.8 12.5 %collective-permute-start.4 = (bf16[2048,640]{0,1:T(8,128)(2,1)}, bf16[2048,640]{0,1:T(8,128)(2,1)}, u32[]{:S(2)}, u32[]{:S(2)}) collective-permute-start(bf16[2048,640]{0,1:T(8,128)(2,1)} %add_convert_fusion), channel_id=1, source_target_pairs={{0,1},{1,0},{2,3},{3,2},{4,5},{5,4},{6,7},{7,6},{8,9},{9,8},{10,11... | collective-permute-start | bytes 7864328 | tf_op jit(solution)/shard_map/ppermute | solution.py:290
  224.0 2.9 copy-start.27
  226.9 2.9 copy-start.50
  236.3 5.9 copy-start.4
  236.3 5.9 copy-start.8
  236.3 5.9 copy-start.10
  249.6 2.3 copy-start.6
  251.9 4.4 copy-start.49
  284.1 18.5 %copy-start.28 = (bf16[2048,256]{0,1:T(8,128)(2,1)}, bf16[2048,256]{0,1:T(8,128)(2,1)S(1)}, u32[]{:S(2)}) copy-start(bf16[2048,256]{0,1:T(8,128)(2,1)S(1)} %copy.158) | copy-start | bytes 3145732
  289.9 3.3 copy-start.22
  289.9 3.3 copy-start.24
  293.2 4.0 copy-start.12
  293.2 4.0 copy-start.31
  293.2 4.0 copy-start.44
  297.8 2.2 copy-start.2
  297.8 2.2 copy-start.33
  297.9 2.2 copy-start.35
  297.9 2.2 copy-start.42
  301.4 1.7 copy-start.20
  301.4 1.7 copy-start.40
  301.4 2.4 copy-start.45
  303.8 5.8 copy-start.38
  318.5 136.2 %all-reduce.8.cloned.1.call-start = ((), (), s32[]{:S(2)}) async-start(), calls=%async_computation.5 | async-start | bytes 204800 | tf_op jit(solution)/shard_map/psum | solution.py:437
  435.8 181.3 %reduce-scatter.5.cloned.1.call-start = ((), (), s32[]{:S(2)}) async-start(), calls=%async_computation.6 | async-start | bytes 8355840 | tf_op jit(solution)/shard_map/reduce_scatter | solution.py:383
  439.4 4.3 collective-permute-start.5
  443.7 3.5 copy-start.25
  443.7 3.5 dynamic-slice-start
  (4 other events, 4.3 us)
Sparse Core Ops, SparseCore 0:
  12.6 63.7 all-gather.2
  89.8 72.3 all-gather.4
  318.7 114.0 reduce-scatter.2
  436.0 18.7 all-reduce.7
  459.9 157.1 reduce-scatter.4
